TPU v7x, 256 devices: a whole 4x4x8 slice. The times are simulated.
256 devices in a mesh: region: 64 (over z, y, x_hi), mp: 4 (over x_lo, core).
Axes of the slice: x: 4 (x_hi: 2, x_lo: 2; x = x_hi * 2 + x_lo), y: 4, z: 8, core: 2. Of those that a mesh axis runs over, the one named last changes fastest.
Arguments:
- features: bfloat16 [32768, 512], P('region'), may hold values from -6 to 6
- neighbours: int32 [32768, 27], P('region'), may hold values from -1 to 1023, as said below
- order: int32 [64, 512], P('region'), may hold values from 0 to 511, each once within a row
- dest: int32 [32768, 1], P('region'), may hold values from 0 to 63; in each aligned block of 512 rows (0 to 511, 512 to 1023, ...) at most 16 rows name the same one
- conv_weight: bfloat16 [27, 512, 512], P(None, None, 'mp'), may hold values from -0.0546875 to 0.0546875
- conv_bias: float32 [512], P('mp'), may hold values from -4 to 4
- cpe_gain: float32 [512], replicated, may hold values from 0.5 to 1.5
- cpe_shift: float32 [512], replicated, may hold values from -3 to 3
- norm1_gain: float32 [512], replicated, may hold values from 0.5 to 1.5
- norm1_shift: float32 [512], replicated, may hold values from -3 to 3
- qkv_weight: bfloat16 [3, 512, 512], P(None, None, 'mp')
- proj_weight: bfloat16 [512, 512], P('mp'), may hold values from -0.25 to 0.25
- proj_bias: float32 [512], replicated, may hold values from -3 to 3
- norm2_gain: float32 [512], replicated, may hold values from 0.5 to 1.5
- norm2_shift: float32 [512], replicated, may hold values from -3 to 3
- fc1_weight: bfloat16 [512, 2048], P(None, 'mp'), may hold values from -0.25 to 0.25
- fc1_bias: float32 [2048], replicated, may hold values from -3 to 3
- fc2_weight: bfloat16 [2048, 512], P('mp'), may hold values from -0.125 to 0.125
- fc2_bias: float32 [512], replicated, may hold values from -3 to 3
Outputs:
- block_out: bfloat16 [32768, 512], P('region')
Inputs may be any that keep to these rules, and one draw needn't show every extreme that they name: `neighbours`: -1 marks an absent neighbour; other values are rows of the region's points extended by 256 rows of each adjacent region, the lower region's first, and lie within 256 rows of the point's own row (256 plus its index in the region); offset 13 is the voxel itself and is never absent. Each row is an order of the region's points, every index once. `dest`: within one region's points no owner is named more than 16 times, and in every draw some region names some owner exactly 16 times.
All inputs are finite; a program needn't handle non-finite values.
Results may differ from a plain program's by a relative error of at most 0.022.
Values may be sent and summed in bfloat16 or wider, within the bound.
A program may use at most 128 MiB of HBM per device.

v0:
```python
import functools
import jax
import jax.numpy as jnp
from jax import lax
from jax.experimental import pallas as pl
from jax.experimental.pallas import tpu as pltpu
from jax.sharding import PartitionSpec as P

HD = 16
RIM = 256
TILE = 128
WINDOW = TILE + 2 * RIM
TAPS = 3
LANES = 128
EMPTY_SCORE = -1e30
MESH = pl.DeviceIdType.MESH
VMEM_LIMIT = 56 * 1024 * 1024
F32 = jnp.float32
BF16 = jnp.bfloat16


def iota(shape, dim):
    return lax.broadcasted_iota(jnp.int32, shape, dim)


def layer_norm(values, scaling, shifting):
    average = jnp.mean(values, axis=-1, keepdims=True)
    centred = values - average
    variance = jnp.mean(centred * centred, axis=-1, keepdims=True)
    return centred * lax.rsqrt(variance + 1e-05) * scaling + shifting


def route(order, dest_row, capacity):
    points = order.shape[1]
    square = (points, points)
    across, down = iota(square, 1), iota(square, 0)
    same = across == down

    def to_row(column):
        return jnp.sum(jnp.where(same, column, 0.0), axis=0, keepdims=True)

    def to_column(row):
        return jnp.sum(jnp.where(same, row, 0.0), axis=1, keepdims=True)

    place = jnp.sum(jnp.where(order == down, across.astype(F32), 0.0), axis=1, keepdims=True)
    dest_row = dest_row.astype(F32)
    dest = to_column(dest_row)
    earlier = (to_row(place) < place) & (dest_row == dest)
    slot = jnp.sum(jnp.where(earlier, 1.0, 0.0), axis=1, keepdims=True)
    position = dest * capacity + slot
    return position.astype(jnp.int32), to_row(position).astype(jnp.int32)


def kernel(
    feat_hbm, links_ref, order_ref, dest_ref, convw_hbm, convb_ref,
    g0, b0, g1, b1, qkv_ref, proj_hbm, bias0, g2, b2, fc1_hbm, bias1, fc2_hbm, bias2,
    out_ref,
    ext, links, acc, lifted, convw, gath, cpe, triple, column, row,
    outgoing, arrived, queries, keys, values, done, returned, held, att, final,
    projs, fc1s, fc2s,
    local_sem, convw_sem, halo_send, halo_recv, conv_send, conv_recv,
    points_send, points_recv, back_send, back_recv, mp_send, mp_recv,
    end_send, end_recv, wt_send, wt_recv,
):
    region, owners = lax.axis_index("region"), lax.axis_size("region")
    mine, parts = lax.axis_index("mp"), lax.axis_size("mp")
    points = feat_hbm.shape[0]
    width = convw.shape[2]
    half = points // 2
    core = lax.rem(mine, 2)
    twin = mine + 1 - 2 * core
    across = lax.rem(mine + 2, 4)
    diagonal = lax.rem(twin + 2, 4)
    above, below = lax.rem(region + 1, owners), lax.rem(region + owners - 1, owners)

    def remote(src, dst, send, recv, **target):
        return pltpu.make_async_remote_copy(
            src_ref=src, dst_ref=dst, send_sem=send, recv_sem=recv,
            device_id=target, device_id_type=MESH,
        )

    own_feat = pltpu.make_async_copy(feat_hbm, ext.at[pl.ds(RIM, points)], local_sem.at[0])
    own_feat.start()

    def weight_chunk(c):
        part = pl.ds(c * TAPS, TAPS)
        return pltpu.make_async_copy(convw_hbm.at[part], convw.at[part], convw_sem.at[c])

    chunks = convw.shape[0] // TAPS

    @pl.loop(0, chunks)
    def _(c):
        weight_chunk(c).start()

    mats = ((proj_hbm, projs), (fc1_hbm, fc1s), (fc2_hbm, fc2s))
    own_mats = [
        pltpu.make_async_copy(hbm, full.at[mine], local_sem.at[1 + i])
        for i, (hbm, full) in enumerate(mats)
    ]
    for copy in own_mats:
        copy.start()

    barrier = pltpu.get_barrier_semaphore()

    @pl.loop(1, owners)
    def _(step):
        pl.semaphore_signal(
            barrier, inc=1, device_id={"region": lax.rem(region + step, owners)},
            device_id_type=MESH,
        )

    for peer in (twin, across, diagonal):
        pl.semaphore_signal(barrier, inc=1, device_id={"mp": peer}, device_id_type=MESH)

    to_column, to_row = route(order_ref[...], dest_ref[...], outgoing.shape[2])
    column[...] = to_column
    row[...] = to_row
    padded = jnp.concatenate(
        [links_ref[...], jnp.zeros((LANES - links_ref.shape[0], points), jnp.int32)], axis=0
    )
    links[...] = padded.T
    acc[...] = jnp.zeros_like(acc) + convb_ref[...]
    pl.semaphore_wait(barrier, owners - 1 + parts - 1)

    rim_half = RIM // 2

    def low_rows(c):
        return ext.at[pl.ds(c * rim_half, rim_half)]

    def high_rows(c):
        return ext.at[pl.ds(RIM + points + c * rim_half, rim_half)]

    up = remote(
        feat_hbm.at[pl.ds(points - RIM + core * rim_half, rim_half)], low_rows(core),
        halo_send.at[0], halo_recv.at[0], region=above,
    )
    down = remote(
        feat_hbm.at[pl.ds(core * rim_half, rim_half)], high_rows(core),
        halo_send.at[1], halo_recv.at[1], region=below,
    )
    up.start()
    down.start()

    def low_forward(c):
        return remote(low_rows(c), low_rows(c), halo_send.at[2], halo_recv.at[2], mp=twin)

    def high_forward(c):
        return remote(high_rows(c), high_rows(c), halo_send.at[3], halo_recv.at[3], mp=twin)

    def lift(c, first, count, keep=None):
        weight = jnp.concatenate([convw[c * TAPS + k] for k in range(TAPS)], axis=1)
        raw = jnp.dot(ext[first : first + count], weight, preferred_element_type=F32)
        lifted[0:count] = (raw if keep is None else raw * keep).astype(BF16)

    def pick(tile, first, low, high):
        here = slice(tile * TILE, (tile + 1) * TILE)
        total = acc[here]
        for k in range(TAPS):
            hit = iota((TILE, high - low), 1) + low == links[here, k : k + 1]
            total += jnp.dot(
                hit.astype(F32).astype(BF16),
                lifted[low - first : high - first, k * width : (k + 1) * width],
                preferred_element_type=F32,
            )
        acc[here] = total

    tiles = points // TILE
    own_feat.wait()

    @pl.loop(0, chunks)
    def _(c):
        weight_chunk(c).wait()
        lift(c, RIM, points)
        for tile in range(tiles):
            low, high = max(RIM, tile * TILE), min(RIM + points, tile * TILE + WINDOW)
            pick(tile, RIM, low, high)
        links[...] = pltpu.roll(links[...], LANES - TAPS, 1)

    def gather_direct(h, peer, slot):
        return remote(
            gath.at[mine, h], gath.at[mine, h],
            conv_send.at[h, slot], conv_recv.at[h, slot], mp=peer,
        )

    def gather_arrival(h, source, slot):
        return remote(
            gath.at[source, h], gath.at[source, h],
            conv_send.at[h, slot], conv_recv.at[h, slot], mp=twin,
        )

    def send_half(h):
        gath[mine, h] = acc[h * half : (h + 1) * half].astype(BF16)
        gather_direct(h, across, 0).start()
        gather_direct(h, twin, 1).start()

    up.wait_recv()
    low_forward(core).start()
    down.wait_recv()
    high_forward(core).start()
    low_forward(1 - core).wait_recv()
    keep_low = jnp.where(region > 0, 1.0, 0.0)

    @pl.loop(0, chunks)
    def _(i):
        links[...] = pltpu.roll(links[...], TAPS, 1)
        lift(chunks - 1 - i, 0, RIM, keep_low)
        for tile in range(RIM // TILE):
            pick(tile, 0, tile * TILE, RIM)

    send_half(0)

    high_forward(1 - core).wait_recv()
    keep_high = jnp.where(region < owners - 1, 1.0, 0.0)
    end = RIM + points

    @pl.loop(0, chunks)
    def _(c):
        lift(c, end, RIM, keep_high)
        for tile in range(tiles - RIM // TILE, tiles):
            pick(tile, end, end, tile * TILE + WINDOW)
        links[...] = pltpu.roll(links[...], LANES - TAPS, 1)

    send_half(1)

    def forward_half(h):
        gather_arrival(h, across, 0).wait_recv()
        remote(
            gath.at[across, h], gath.at[across, h],
            conv_send.at[h, 2], conv_recv.at[h, 2], mp=twin,
        ).start()

    forward_half(0)

    weight_qkv = jnp.concatenate([qkv_ref[i] for i in range(3)], axis=1)
    for h in range(2):
        if h == 1:
            forward_half(1)
        gather_arrival(h, twin, 1).wait_recv()
        gather_arrival(h, diagonal, 2).wait_recv()
        here = slice(h * half, (h + 1) * half)
        conv = jnp.concatenate([gath[i, h] for i in range(parts)], axis=1).astype(F32)
        mixed = ext[RIM + h * half : RIM + (h + 1) * half].astype(F32) + layer_norm(
            conv, g0[...], b0[...]
        )
        cpe[here] = mixed.astype(BF16)
        normed = layer_norm(cpe[here].astype(F32), g1[...], b1[...]).astype(BF16)
        triple[here] = jnp.dot(normed, weight_qkv, preferred_element_type=F32).astype(BF16)

    outer, inner, capacity = outgoing.shape[0], outgoing.shape[1], outgoing.shape[2]
    group = outer * capacity
    own_outer, own_inner = region // inner, lax.rem(region, inner)

    def points_copy(a, t, target, arrival):
        other = a * inner + t
        slot = other if arrival else region
        return remote(
            outgoing.at[a, t], arrived.at[slot // inner, lax.rem(slot, inner)],
            points_send.at[target], points_recv.at[slot], region=other,
        )

    @pl.loop(0, inner)
    def _(t):
        at = iota((group, points), 0)
        slot = (at // capacity) * (inner * capacity) + t * capacity + lax.rem(at, capacity)
        hit = (slot == row[...]).astype(F32)
        filled = jnp.sum(hit, axis=1, keepdims=True) > 0
        moved = jnp.dot(hit.astype(BF16), triple[...], preferred_element_type=F32)
        query = jnp.where(filled, moved[:, :width] * HD ** (-0.5), jnp.inf).astype(BF16)
        outgoing[:, t, :, :width] = query.reshape(outer, capacity, width)
        outgoing[:, t, :, width:] = (
            moved[:, width:].astype(BF16).reshape(outer, capacity, 2 * width)
        )

        @pl.loop(0, outer)
        def _(i):
            a = lax.rem(i + own_outer, outer)
            other = a * inner + t

            @pl.when(other != region)
            def _():
                points_copy(a, t, other, False).start()

    arrived[own_outer, own_inner] = outgoing[own_outer, own_inner]

    def mat(i, part, slot, peer):
        full = mats[i][1]
        return remote(
            full.at[part], full.at[part], wt_send.at[i, slot], wt_recv.at[i, slot], mp=peer
        )

    for copy in own_mats:
        copy.wait()
    for i in range(3):
        mat(i, mine, 0, across).start()
    for i in range(3):
        mat(i, mine, 1, twin).start()

    def every_other(body):
        @pl.loop(0, owners)
        def _(s):
            @pl.when(s != region)
            def _():
                body(s)

    every_other(lambda s: points_copy(s // inner, lax.rem(s, inner), s, True).wait_recv())

    heads = width // HD
    rows = owners * capacity
    whole = arrived[...].reshape(rows, 3 * width)
    query = whole[:, :width].astype(F32)
    empty = query[:, 0:1] == jnp.inf
    one = jnp.where(iota((rows, width), 1) == 0, 1.0, 0.0)
    queries[:, :, :, :width] = (
        jnp.where(empty, 0.0, query).astype(BF16).reshape(outer, inner, capacity, width)
    )
    queries[:, :, :, width:] = one.astype(BF16).reshape(outer, inner, capacity, width)
    keys[:width] = whole[:, width : 2 * width].T
    keys[width:] = (jnp.where(empty, EMPTY_SCORE, 0.0) * one).T.astype(BF16)
    value = whole[:, 2 * width :]
    value_lane = iota((rows, width), 1) // HD
    for head in range(heads):
        here = jnp.where(value_lane == head, 1.0, 0.0).astype(BF16)
        values[head, :, :width] = value * here
        values[head, :, width:] = here

    def back_copy(a, t, target, arrival):
        other = a * inner + t
        slot = other if arrival else region
        return remote(
            done.at[a, t], returned.at[slot // inner, lax.rem(slot, inner)],
            back_send.at[target], back_recv.at[slot], region=other,
        )

    @pl.loop(0, inner)
    def _(t):
        query = queries[:, t].reshape(group, 2 * width)
        lane = iota((group, 2 * width), 1)
        total = jnp.zeros((group, 2 * width), F32)
        for head in range(heads):
            keep = ((lane // HD) == head) | (lane >= width)
            own = query * jnp.where(keep, 1.0, 0.0).astype(BF16)
            scores = jnp.dot(own, keys[...], preferred_element_type=F32)
            peak = jnp.max(scores, axis=1, keepdims=True)
            raised = jnp.exp(scores - peak).astype(BF16)
            total += jnp.dot(raised, values[head], preferred_element_type=F32)
        done[:, t] = (
            (total[:, :width] / total[:, width:]).astype(BF16).reshape(outer, capacity, width)
        )

        @pl.loop(0, outer)
        def _(i):
            a = lax.rem(i + own_outer, outer)
            other = a * inner + t

            @pl.when(other != region)
            def _():
                back_copy(a, t, other, False).start()

    returned[own_outer, own_inner] = done[own_outer, own_inner]

    for i in range(3):
        mat(i, across, 0, twin).wait_recv()
        mat(i, across, 2, twin).start()

    every_other(lambda s: back_copy(s // inner, lax.rem(s, inner), s, True).wait_recv())

    hit = (iota((points, rows), 1) == column[...]).astype(F32).astype(BF16)
    moved = jnp.dot(
        hit, returned[...].reshape(rows, width), preferred_element_type=F32
    ).astype(BF16)
    share = points // parts
    for part in range(parts):
        held[part] = moved[part * share : (part + 1) * share]

    peers = (twin, across, diagonal)

    def held_copy(i, peer, arrival):
        return remote(
            held.at[peer], att.at[peer if arrival else mine], mp_send.at[i], mp_recv.at[i], mp=peer
        )

    for i, peer in enumerate(peers):
        held_copy(i, peer, False).start()
    att[mine] = held[mine]
    for i in range(3):
        mat(i, twin, 1, twin).wait_recv()
        mat(i, diagonal, 2, twin).wait_recv()
    for i, peer in enumerate(peers):
        held_copy(i, peer, True).wait_recv()

    heads_out = jnp.concatenate([att[i] for i in range(parts)], axis=1)
    own_rows = pl.ds(pl.multiple_of(mine * share, share), share)
    after = (
        cpe[own_rows].astype(F32)
        + jnp.dot(heads_out, projs[...].reshape(points, points), preferred_element_type=F32)
        + bias0[...]
    ).astype(BF16)
    normed = layer_norm(after.astype(F32), g2[...], b2[...]).astype(BF16)
    total = after.astype(F32) + bias2[...]
    wide = fc1s.shape[2]
    for i in range(parts):
        raw = jnp.dot(normed, fc1s[i], preferred_element_type=F32)
        raw += bias1[:, i * wide : (i + 1) * wide]
        hidden = (0.5 * raw * (1.0 + lax.erf(raw * (0.5**0.5)))).astype(BF16)
        total += jnp.dot(hidden, fc2s[i], preferred_element_type=F32)
    final[mine] = total.astype(BF16)

    def end_copy(i, peer, arrival):
        slot = peer if arrival else mine
        return remote(
            final.at[slot], final.at[slot], end_send.at[i], end_recv.at[i], mp=peer
        )

    for i, peer in enumerate(peers):
        end_copy(i, peer, False).start()

    up.wait_send()
    down.wait_send()
    low_forward(core).wait_send()
    high_forward(core).wait_send()
    for h in range(2):
        for slot in range(3):
            gather_direct(h, twin, slot).wait_send()
    every_other(lambda s: points_copy(s // inner, lax.rem(s, inner), s, False).wait_send())
    every_other(lambda s: back_copy(s // inner, lax.rem(s, inner), s, False).wait_send())
    for i in range(3):
        for slot in range(3):
            mat(i, mine, slot, twin).wait_send()
    for i, peer in enumerate(peers):
        held_copy(i, peer, False).wait_send()

    for i, peer in enumerate(peers):
        end_copy(i, peer, True).wait_recv()
    for i, peer in enumerate(peers):
        end_copy(i, peer, False).wait_send()
    out_ref[...] = final[...].reshape(out_ref.shape)


def local(
    features, neighbours, order, dest, conv_weight, conv_bias,
    cpe_gain, cpe_shift, norm1_gain, norm1_shift, qkv_weight, proj_weight, proj_bias,
    norm2_gain, norm2_shift, fc1_weight, fc1_bias, fc2_weight, fc2_bias,
):
    points, channels = features.shape
    owners = lax.axis_size("region")
    parts = lax.axis_size("mp")
    capacity = 2 * points // owners
    inner = 4
    outer = owners // inner
    taps, _, width = conv_weight.shape
    rows = owners * capacity
    half = points // 2
    share = points // parts
    heads = width // HD
    wide = fc1_weight.shape[1]
    line = lambda x: x.reshape(1, -1)
    vmem = pl.BlockSpec(memory_space=pltpu.VMEM)
    hbm = pl.BlockSpec(memory_space=pl.ANY)
    blocks = (outer, inner, capacity)
    dma = pltpu.SemaphoreType.DMA
    return pl.pallas_call(
        kernel,
        out_shape=jax.ShapeDtypeStruct(features.shape, BF16),
        in_specs=[
            hbm, vmem, vmem, vmem, hbm, vmem,
            vmem, vmem, vmem, vmem, vmem, hbm, vmem, vmem, vmem, hbm, vmem, hbm, vmem,
        ],
        out_specs=vmem,
        scratch_shapes=[
            pltpu.VMEM((points + 2 * RIM, channels), BF16),
            pltpu.VMEM((points, LANES), jnp.int32),
            pltpu.VMEM((points, width), F32),
            pltpu.VMEM((points, TAPS * width), BF16),
            pltpu.VMEM((taps, channels, width), BF16),
            pltpu.VMEM((parts, 2, half, width), BF16),
            pltpu.VMEM((points, channels), BF16),
            pltpu.VMEM((points, 3 * width), BF16),
            pltpu.VMEM((points, 1), jnp.int32),
            pltpu.VMEM((1, points), jnp.int32),
            pltpu.VMEM(blocks + (3 * width,), BF16),
            pltpu.VMEM(blocks + (3 * width,), BF16),
            pltpu.VMEM(blocks + (2 * width,), BF16),
            pltpu.VMEM((2 * width, rows), BF16),
            pltpu.VMEM((heads, rows, 2 * width), BF16),
            pltpu.VMEM(blocks + (width,), BF16),
            pltpu.VMEM(blocks + (width,), BF16),
            pltpu.VMEM((parts, share, width), BF16),
            pltpu.VMEM((parts, share, width), BF16),
            pltpu.VMEM((parts, share, channels), BF16),
            pltpu.VMEM((parts,) + proj_weight.shape, BF16),
            pltpu.VMEM((parts,) + fc1_weight.shape, BF16),
            pltpu.VMEM((parts,) + fc2_weight.shape, BF16),
            dma((4,)), dma((taps // TAPS,)), dma((4,)), dma((4,)), dma((2, 3)), dma((2, 3)),
            dma((owners,)), dma((owners,)), dma((owners,)), dma((owners,)), dma((3,)), dma((3,)),
            dma((3,)), dma((3,)), dma((3, 3)), dma((3, 3)),
        ],
        compiler_params=pltpu.CompilerParams(
            collective_id=0, has_side_effects=True, vmem_limit_bytes=VMEM_LIMIT
        ),
        name="block",
    )(
        features, neighbours.T, order, dest.T, conv_weight, line(conv_bias),
        line(cpe_gain), line(cpe_shift), line(norm1_gain), line(norm1_shift), qkv_weight,
        proj_weight, line(proj_bias), line(norm2_gain), line(norm2_shift),
        fc1_weight, line(fc1_bias), fc2_weight, line(fc2_bias),
    )


def solution(mesh):
    row = P("region", None)
    placed = (
        row, row, row, row, P(None, None, "mp"), P("mp"),
        P(), P(), P(), P(), P(None, None, "mp"), P("mp", None), P(),
        P(), P(), P(None, "mp"), P(), P("mp", None), P(),
    )
    return jax.shard_map(
        local, mesh=mesh, in_specs=placed, out_specs=P("region", None), check_vma=False
    )
```

profile of v0, /device:TPU:15, one launch (start us, length us, event | category | flops | bytes accessed | tf_op | source)
XLA Modules:
  0.0 100.5 jit_solution(8506368287506920918)
XLA Ops:
  0.0 98.6 %block.1 = bf16[512,512]{1,0:T(8,128)(2,1)} custom-call(bf16[512,512]{1,0:T(8,128)(2,1)} %feat_hbm.1, s32[27,512]{1,0:T(8,128)} %bitcast.12, s32[1,512]{1,0:T(1,128)} %order_ref.1, s32[1,512]{1,0:T(1,128)} %bitcast.14, bf16[27,512,128]{2,1,0:T(8,128)(2,1)} %convw_hbm.1, f32[1,128]{1,0:T(1,128)} %bitcast.23, f32[1,512]{1,0:T(1,128)} %bitcast.15, ...), custom_call_target="tpu_custom_call" | custom-call | tf_op jit(solution)/shard_map/block/pallas_call | solution.py:461
  98.6 1.9 %copy.21 = bf16[512,512]{1,0:T(8,128)(2,1)} copy(bf16[512,512]{1,0:T(8,128)(2,1)} %block.1) | data formatting | bytes 1048576
where the time goes:
time: 101 us; the launch traced here: 100 us
  Pallas kernels  98.6 us (98%)
  local copies, waits for them, and re-layouts  1.87 us (2%)
    pallas_call x1, Pallas kernels, local(): pl.pallas_call(kernel, out_shape=jax.ShapeDtypeStruct(features.shape, BF1...  98.6 us

commit v1 on v0

--- a/solution.py
+++ b/solution.py
@@ -1,4 +1,5 @@
-import functools
+import math
+
 import jax
 import jax.numpy as jnp
 from jax import lax
@@ -10,9 +11,11 @@
 RIM = 256
 TILE = 128
 WINDOW = TILE + 2 * RIM
-TAPS = 3
+TAPS = 9
+EARLY_CHUNK = 1
 LANES = 128
 EMPTY_SCORE = -1e30
+SCORE_SCALE = HD ** (-0.5) * math.log2(math.e)
 MESH = pl.DeviceIdType.MESH
 VMEM_LIMIT = 56 * 1024 * 1024
 F32 = jnp.float32
@@ -56,7 +59,7 @@
     g0, b0, g1, b1, qkv_ref, proj_hbm, bias0, g2, b2, fc1_hbm, bias1, fc2_hbm, bias2,
     out_ref,
     ext, links, acc, lifted, convw, gath, cpe, triple, column, row,
-    outgoing, arrived, queries, keys, values, done, returned, held, att, final,
+    outgoing, arrived, outgoing2, arrived2, queries, keys, values, firsts, blank, done, returned, held, att, final,
     projs, fc1s, fc2s,
     local_sem, convw_sem, halo_send, halo_recv, conv_send, conv_recv,
     points_send, points_recv, back_send, back_recv, mp_send, mp_recv,
@@ -93,6 +96,33 @@
         weight_chunk(c).start()
 
     mats = ((proj_hbm, projs), (fc1_hbm, fc1s), (fc2_hbm, fc2s))
+    split = fc1s.shape[1] // 2
+    pieces = (
+        (projs, pl.ds(0, projs.shape[1])),
+        (fc1s, pl.ds(0, split)),
+        (fc1s, pl.ds(split, split)),
+        (fc2s, pl.ds(0, fc2s.shape[1])),
+    )
+    early, late = (0, 1), (2, 3)
+
+    def mat(i, part, slot, peer):
+        full, where = pieces[i]
+        return remote(
+            full.at[part, where], full.at[part, where],
+            wt_send.at[i, slot], wt_recv.at[i, slot], mp=peer,
+        )
+
+    def mats_out(which):
+        for i in which:
+            mat(i, mine, 0, across).start()
+        for i in which:
+            mat(i, mine, 1, twin).start()
+
+    def mats_on(which):
+        for i in which:
+            mat(i, across, 0, twin).wait_recv()
+            mat(i, across, 2, twin).start()
+
     own_mats = [
         pltpu.make_async_copy(hbm, full.at[mine], local_sem.at[1 + i])
         for i, (hbm, full) in enumerate(mats)
@@ -112,9 +142,6 @@
     for peer in (twin, across, diagonal):
         pl.semaphore_signal(barrier, inc=1, device_id={"mp": peer}, device_id_type=MESH)
 
-    to_column, to_row = route(order_ref[...], dest_ref[...], outgoing.shape[2])
-    column[...] = to_column
-    row[...] = to_row
     padded = jnp.concatenate(
         [links_ref[...], jnp.zeros((LANES - links_ref.shape[0], points), jnp.int32)], axis=0
     )
@@ -167,8 +194,15 @@
     tiles = points // TILE
     own_feat.wait()
 
+    for copy in own_mats:
+        copy.wait()
+
     @pl.loop(0, chunks)
     def _(c):
+        @pl.when(c == EARLY_CHUNK)
+        def _():
+            mats_out(early)
+
         weight_chunk(c).wait()
         lift(c, RIM, points)
         for tile in range(tiles):
@@ -231,10 +265,13 @@
 
     forward_half(0)
 
+    to_column, to_row = route(order_ref[...], dest_ref[...], outgoing.shape[2])
+    column[...] = to_column
+    row[...] = to_row
+    forward_half(1)
+
     weight_qkv = jnp.concatenate([qkv_ref[i] for i in range(3)], axis=1)
     for h in range(2):
-        if h == 1:
-            forward_half(1)
         gather_arrival(h, twin, 1).wait_recv()
         gather_arrival(h, diagonal, 2).wait_recv()
         here = slice(h * half, (h + 1) * half)
@@ -244,19 +281,37 @@
         )
         cpe[here] = mixed.astype(BF16)
         normed = layer_norm(cpe[here].astype(F32), g1[...], b1[...]).astype(BF16)
-        triple[here] = jnp.dot(normed, weight_qkv, preferred_element_type=F32).astype(BF16)
+        raw = jnp.dot(normed, weight_qkv, preferred_element_type=F32)
+        query = (raw[:, :width] * SCORE_SCALE).astype(BF16)
+        key = raw[:, width : 2 * width].astype(BF16)
+        side = width // 2
+        triple[here, :width] = jnp.concatenate([query[:, :side], key[:, :side]], axis=1)
+        triple[here, width : 2 * width] = raw[:, 2 * width :].astype(BF16)
+        triple[here, 2 * width :] = jnp.concatenate([query[:, side:], key[:, side:]], axis=1)
 
     outer, inner, capacity = outgoing.shape[0], outgoing.shape[1], outgoing.shape[2]
     group = outer * capacity
     own_outer, own_inner = region // inner, lax.rem(region, inner)
 
-    def points_copy(a, t, target, arrival):
+    def points_copy(first, a, t, target, arrival):
         other = a * inner + t
         slot = other if arrival else region
+        src, dst = (outgoing, arrived) if first else (outgoing2, arrived2)
+        kind = 0 if first else 1
         return remote(
-            outgoing.at[a, t], arrived.at[slot // inner, lax.rem(slot, inner)],
-            points_send.at[target], points_recv.at[slot], region=other,
-        )
+            src.at[a, t], dst.at[slot // inner, lax.rem(slot, inner)],
+            points_send.at[kind, target], points_recv.at[kind, slot], region=other,
+        )
+
+    def points_out(first, t):
+        @pl.loop(0, outer)
+        def _(i):
+            a = lax.rem(i + own_outer, outer)
+            other = a * inner + t
+
+            @pl.when(other != region)
+            def _():
+                points_copy(first, a, t, other, False).start()
 
     @pl.loop(0, inner)
     def _(t):
@@ -265,35 +320,23 @@
         hit = (slot == row[...]).astype(F32)
         filled = jnp.sum(hit, axis=1, keepdims=True) > 0
         moved = jnp.dot(hit.astype(BF16), triple[...], preferred_element_type=F32)
-        query = jnp.where(filled, moved[:, :width] * HD ** (-0.5), jnp.inf).astype(BF16)
-        outgoing[:, t, :, :width] = query.reshape(outer, capacity, width)
+        pair = jnp.where(filled, moved[:, :width], jnp.inf).astype(BF16)
+        outgoing[:, t, :, :width] = pair.reshape(outer, capacity, width)
         outgoing[:, t, :, width:] = (
-            moved[:, width:].astype(BF16).reshape(outer, capacity, 2 * width)
-        )
-
-        @pl.loop(0, outer)
-        def _(i):
-            a = lax.rem(i + own_outer, outer)
-            other = a * inner + t
-
-            @pl.when(other != region)
-            def _():
-                points_copy(a, t, other, False).start()
+            moved[:, width : 2 * width].astype(BF16).reshape(outer, capacity, width)
+        )
+        outgoing2[:, t] = moved[:, 2 * width :].astype(BF16).reshape(outer, capacity, width)
+        points_out(True, t)
+
+    @pl.loop(0, inner)
+    def _(t):
+        points_out(False, t)
 
     arrived[own_outer, own_inner] = outgoing[own_outer, own_inner]
-
-    def mat(i, part, slot, peer):
-        full = mats[i][1]
-        return remote(
-            full.at[part], full.at[part], wt_send.at[i, slot], wt_recv.at[i, slot], mp=peer
-        )
-
-    for copy in own_mats:
-        copy.wait()
-    for i in range(3):
-        mat(i, mine, 0, across).start()
-    for i in range(3):
-        mat(i, mine, 1, twin).start()
+    arrived2[own_outer, own_inner] = outgoing2[own_outer, own_inner]
+
+    mats_out(late)
+    mats_on(early)
 
     def every_other(body):
         @pl.loop(0, owners)
@@ -302,26 +345,63 @@
             def _():
                 body(s)
 
-    every_other(lambda s: points_copy(s // inner, lax.rem(s, inner), s, True).wait_recv())
-
     heads = width // HD
     rows = owners * capacity
-    whole = arrived[...].reshape(rows, 3 * width)
-    query = whole[:, :width].astype(F32)
-    empty = query[:, 0:1] == jnp.inf
-    one = jnp.where(iota((rows, width), 1) == 0, 1.0, 0.0)
-    queries[:, :, :, :width] = (
-        jnp.where(empty, 0.0, query).astype(BF16).reshape(outer, inner, capacity, width)
-    )
-    queries[:, :, :, width:] = one.astype(BF16).reshape(outer, inner, capacity, width)
-    keys[:width] = whole[:, width : 2 * width].T
-    keys[width:] = (jnp.where(empty, EMPTY_SCORE, 0.0) * one).T.astype(BF16)
-    value = whole[:, 2 * width :]
+    side = width // 2
+    near = heads // 2
+
+    def prepare(kind, pairs, empty):
+        lane = iota((rows, width), 1)
+        marked = jnp.where(lane == side, 1.0, 0.0)
+        pairs = jnp.where(empty, 0.0, pairs.astype(F32))
+        query = jnp.where(lane < side, pairs, marked)
+        queries[kind] = query.astype(BF16).reshape(inner, group, width)
+        key = jnp.where(lane < side, pltpu.roll(pairs, side, 1), marked * bias_of(empty))
+        keys[kind] = key.astype(BF16).T
+
+    def bias_of(empty):
+        return jnp.where(empty, EMPTY_SCORE, 0.0)
+
+    every_other(
+        lambda s: points_copy(True, s // inner, lax.rem(s, inner), s, True).wait_recv()
+    )
+    whole = jnp.concatenate([arrived[:, t].reshape(group, 2 * width) for t in range(inner)], axis=0)
+    empty = whole[:, 0:1].astype(F32) == jnp.inf
+    prepare(0, whole[:, :width], empty)
+    blank[...] = jnp.where(empty, 1.0, 0.0)
+    value = whole[:, width:]
     value_lane = iota((rows, width), 1) // HD
     for head in range(heads):
-        here = jnp.where(value_lane == head, 1.0, 0.0).astype(BF16)
-        values[head, :, :width] = value * here
-        values[head, :, width:] = here
+        mask = jnp.where(value_lane == head, 1.0, 0.0).astype(BF16)
+        values[head, :, :width] = value * mask
+        values[head, :, width:] = mask
+
+    def attend(kind, t):
+        query = queries[kind, t]
+        lane = iota((group, width), 1)
+        total = jnp.zeros((group, 2 * width), F32)
+        for head in range(near):
+            keep = ((lane // HD) == head) | (lane >= side)
+            own = query * jnp.where(keep, 1.0, 0.0).astype(BF16)
+            scores = jnp.dot(own, keys[kind], preferred_element_type=F32)
+            peak = jnp.max(scores, axis=1, keepdims=True)
+            raised = jnp.exp2(scores - peak).astype(BF16)
+            total += jnp.dot(raised, values[kind * near + head], preferred_element_type=F32)
+        here = (lane // side) == kind
+        return jnp.where(here, total[:, :width] / jnp.where(here, total[:, width:], 1.0), 0.0)
+
+    @pl.loop(0, inner)
+    def _(t):
+        firsts[t] = attend(0, t)
+
+    every_other(
+        lambda s: points_copy(False, s // inner, lax.rem(s, inner), s, True).wait_recv()
+    )
+    prepare(
+        1,
+        jnp.concatenate([arrived2[:, t].reshape(group, width) for t in range(inner)], axis=0),
+        blank[...] > 0,
+    )
 
     def back_copy(a, t, target, arrival):
         other = a * inner + t
@@ -333,19 +413,7 @@
 
     @pl.loop(0, inner)
     def _(t):
-        query = queries[:, t].reshape(group, 2 * width)
-        lane = iota((group, 2 * width), 1)
-        total = jnp.zeros((group, 2 * width), F32)
-        for head in range(heads):
-            keep = ((lane // HD) == head) | (lane >= width)
-            own = query * jnp.where(keep, 1.0, 0.0).astype(BF16)
-            scores = jnp.dot(own, keys[...], preferred_element_type=F32)
-            peak = jnp.max(scores, axis=1, keepdims=True)
-            raised = jnp.exp(scores - peak).astype(BF16)
-            total += jnp.dot(raised, values[head], preferred_element_type=F32)
-        done[:, t] = (
-            (total[:, :width] / total[:, width:]).astype(BF16).reshape(outer, capacity, width)
-        )
+        done[:, t] = (firsts[t] + attend(1, t)).astype(BF16).reshape(outer, capacity, width)
 
         @pl.loop(0, outer)
         def _(i):
@@ -358,9 +426,7 @@
 
     returned[own_outer, own_inner] = done[own_outer, own_inner]
 
-    for i in range(3):
-        mat(i, across, 0, twin).wait_recv()
-        mat(i, across, 2, twin).start()
+    mats_on(late)
 
     every_other(lambda s: back_copy(s // inner, lax.rem(s, inner), s, True).wait_recv())
 
@@ -382,7 +448,7 @@
     for i, peer in enumerate(peers):
         held_copy(i, peer, False).start()
     att[mine] = held[mine]
-    for i in range(3):
+    for i in range(4):
         mat(i, twin, 1, twin).wait_recv()
         mat(i, diagonal, 2, twin).wait_recv()
     for i, peer in enumerate(peers):
@@ -405,14 +471,22 @@
         total += jnp.dot(hidden, fc2s[i], preferred_element_type=F32)
     final[mine] = total.astype(BF16)
 
-    def end_copy(i, peer, arrival):
-        slot = peer if arrival else mine
+    part_rows = share // 2
+
+    def end_copy(part, piece, slot, peer):
+        where = pl.ds(piece * part_rows, part_rows)
         return remote(
-            final.at[slot], final.at[slot], end_send.at[i], end_recv.at[i], mp=peer
-        )
-
-    for i, peer in enumerate(peers):
-        end_copy(i, peer, False).start()
+            final.at[part, where], final.at[part, where],
+            end_send.at[piece, slot], end_recv.at[piece, slot], mp=peer,
+        )
+
+    for piece in range(2):
+        end_copy(mine, piece, 0, across).start()
+    for piece in range(2):
+        end_copy(mine, piece, 1, twin).start()
+    for piece in range(2):
+        end_copy(across, piece, 0, twin).wait_recv()
+        end_copy(across, piece, 2, twin).start()
 
     up.wait_send()
     down.wait_send()
@@ -421,18 +495,23 @@
     for h in range(2):
         for slot in range(3):
             gather_direct(h, twin, slot).wait_send()
-    every_other(lambda s: points_copy(s // inner, lax.rem(s, inner), s, False).wait_send())
+    for first in (True, False):
+        every_other(
+            lambda s: points_copy(first, s // inner, lax.rem(s, inner), s, False).wait_send()
+        )
     every_other(lambda s: back_copy(s // inner, lax.rem(s, inner), s, False).wait_send())
-    for i in range(3):
+    for i in range(4):
         for slot in range(3):
             mat(i, mine, slot, twin).wait_send()
     for i, peer in enumerate(peers):
         held_copy(i, peer, False).wait_send()
 
-    for i, peer in enumerate(peers):
-        end_copy(i, peer, True).wait_recv()
-    for i, peer in enumerate(peers):
-        end_copy(i, peer, False).wait_send()
+    for piece in range(2):
+        end_copy(twin, piece, 1, twin).wait_recv()
+        end_copy(diagonal, piece, 2, twin).wait_recv()
+    for piece in range(2):
+        for slot in range(3):
+            end_copy(mine, piece, slot, twin).wait_send()
     out_ref[...] = final[...].reshape(out_ref.shape)
 
 
@@ -477,11 +556,15 @@
             pltpu.VMEM((points, 3 * width), BF16),
             pltpu.VMEM((points, 1), jnp.int32),
             pltpu.VMEM((1, points), jnp.int32),
-            pltpu.VMEM(blocks + (3 * width,), BF16),
-            pltpu.VMEM(blocks + (3 * width,), BF16),
             pltpu.VMEM(blocks + (2 * width,), BF16),
-            pltpu.VMEM((2 * width, rows), BF16),
+            pltpu.VMEM(blocks + (2 * width,), BF16),
+            pltpu.VMEM(blocks + (width,), BF16),
+            pltpu.VMEM(blocks + (width,), BF16),
+            pltpu.VMEM((2, inner, outer * capacity, width), BF16),
+            pltpu.VMEM((2, width, rows), BF16),
             pltpu.VMEM((heads, rows, 2 * width), BF16),
+            pltpu.VMEM((inner, outer * capacity, width), F32),
+            pltpu.VMEM((rows, 1), F32),
             pltpu.VMEM(blocks + (width,), BF16),
             pltpu.VMEM(blocks + (width,), BF16),
             pltpu.VMEM((parts, share, width), BF16),
@@ -491,8 +574,8 @@
             pltpu.VMEM((parts,) + fc1_weight.shape, BF16),
             pltpu.VMEM((parts,) + fc2_weight.shape, BF16),
             dma((4,)), dma((taps // TAPS,)), dma((4,)), dma((4,)), dma((2, 3)), dma((2, 3)),
-            dma((owners,)), dma((owners,)), dma((owners,)), dma((owners,)), dma((3,)), dma((3,)),
-            dma((3,)), dma((3,)), dma((3, 3)), dma((3, 3)),
+            dma((2, owners)), dma((2, owners)), dma((owners,)), dma((owners,)), dma((3,)), dma((3,)),
+            dma((2, 3)), dma((2, 3)), dma((4, 3)), dma((4, 3)),
         ],
         compiler_params=pltpu.CompilerParams(
             collective_id=0, has_side_effects=True, vmem_limit_bytes=VMEM_LIMIT

time: 101 us -> 94.2 us (0.933)
  Pallas kernels: 98.6 us -> 92 us
    pallas_call x1, Pallas kernels: 98.6 us -> 92 us  [local(): pl.pallas_call(kernel, out_shape=jax.ShapeDtypeStruct(features.shape, BF1...]
where the time goes in v1:
time: 94.2 us; the launch traced here: 93.9 us
  Pallas kernels  92 us (98%)
  local copies, waits for them, and re-layouts  1.87 us (2%)
    pallas_call x1, Pallas kernels, local(): pl.pallas_call(kernel, out_shape=jax.ShapeDtypeStruct(features.shape, BF1...  92 us

profile of v1, /device:TPU:15, one launch (start us, length us, event | category | flops | bytes accessed | tf_op | source)
XLA Modules:
  0.0 93.9 jit_solution(17536954418429565555)
XLA Ops:
  0.0 92.0 %block.1 = bf16[512,512]{1,0:T(8,128)(2,1)} custom-call(bf16[512,512]{1,0:T(8,128)(2,1)} %feat_hbm.1, s32[27,512]{1,0:T(8,128)} %bitcast.12, s32[1,512]{1,0:T(1,128)} %order_ref.1, s32[1,512]{1,0:T(1,128)} %bitcast.14, bf16[27,512,128]{2,1,0:T(8,128)(2,1)} %convw_hbm.1, f32[1,128]{1,0:T(1,128)} %bitcast.23, f32[1,512]{1,0:T(1,128)} %bitcast.15, ...), custom_call_target="tpu_custom_call" | custom-call | tf_op jit(solution)/shard_map/block/pallas_call | solution.py:540
  92.0 1.9 %copy.21 = bf16[512,512]{1,0:T(8,128)(2,1)} copy(bf16[512,512]{1,0:T(8,128)(2,1)} %block.1) | data formatting | bytes 1048576

commit v2 on v1

--- a/solution.py
+++ b/solution.py
@@ -12,7 +12,6 @@
 TILE = 128
 WINDOW = TILE + 2 * RIM
 TAPS = 9
-EARLY_CHUNK = 1
 LANES = 128
 EMPTY_SCORE = -1e30
 SCORE_SCALE = HD ** (-0.5) * math.log2(math.e)
@@ -59,7 +58,7 @@
     g0, b0, g1, b1, qkv_ref, proj_hbm, bias0, g2, b2, fc1_hbm, bias1, fc2_hbm, bias2,
     out_ref,
     ext, links, acc, lifted, convw, gath, cpe, triple, column, row,
-    outgoing, arrived, outgoing2, arrived2, queries, keys, values, firsts, blank, done, returned, held, att, final,
+    outgoing, arrived, outgoing2, arrived2, queries, keys, values, firsts, blank, collecting, done, returned, held, att, final,
     projs, fc1s, fc2s,
     local_sem, convw_sem, halo_send, halo_recv, conv_send, conv_recv,
     points_send, points_recv, back_send, back_recv, mp_send, mp_recv,
@@ -199,10 +198,6 @@
 
     @pl.loop(0, chunks)
     def _(c):
-        @pl.when(c == EARLY_CHUNK)
-        def _():
-            mats_out(early)
-
         weight_chunk(c).wait()
         lift(c, RIM, points)
         for tile in range(tiles):
@@ -335,8 +330,8 @@
     arrived[own_outer, own_inner] = outgoing[own_outer, own_inner]
     arrived2[own_outer, own_inner] = outgoing2[own_outer, own_inner]
 
+    mats_out(early)
     mats_out(late)
-    mats_on(early)
 
     def every_other(body):
         @pl.loop(0, owners)
@@ -425,14 +420,15 @@
                 back_copy(a, t, other, False).start()
 
     returned[own_outer, own_inner] = done[own_outer, own_inner]
-
+    collecting[...] = (iota((points, rows), 1) == column[...]).astype(F32).astype(BF16)
+
+    mats_on(early)
     mats_on(late)
 
     every_other(lambda s: back_copy(s // inner, lax.rem(s, inner), s, True).wait_recv())
 
-    hit = (iota((points, rows), 1) == column[...]).astype(F32).astype(BF16)
     moved = jnp.dot(
-        hit, returned[...].reshape(rows, width), preferred_element_type=F32
+        collecting[...], returned[...].reshape(rows, width), preferred_element_type=F32
     ).astype(BF16)
     share = points // parts
     for part in range(parts):
@@ -565,6 +561,7 @@
             pltpu.VMEM((heads, rows, 2 * width), BF16),
             pltpu.VMEM((inner, outer * capacity, width), F32),
             pltpu.VMEM((rows, 1), F32),
+            pltpu.VMEM((points, rows), BF16),
             pltpu.VMEM(blocks + (width,), BF16),
             pltpu.VMEM(blocks + (width,), BF16),
             pltpu.VMEM((parts, share, width), BF16),

time: 94.2 us -> 93.1 us (0.988)
  the two profiles are of different devices: /device:TPU:15 before, /device:TPU:1 now
where the time goes in v2:
time: 93.1 us; the launch traced here: 92.9 us
  Pallas kernels  91 us (98%)
  local copies, waits for them, and re-layouts  1.87 us (2%)
    pallas_call x1, Pallas kernels, local(): pl.pallas_call(kernel, out_shape=jax.ShapeDtypeStruct(features.shape, BF1...  91 us
    unnamed x1, local copies, waits for them, and re-layouts  1.87 us

profile of v2, /device:TPU:1, one launch (start us, length us, event | category | flops | bytes accessed | tf_op | source)
XLA Modules:
  0.0 92.9 jit_solution(6483456082109335019)
XLA Ops:
  0.0 91.0 %block.1 = bf16[512,512]{1,0:T(8,128)(2,1)} custom-call(bf16[512,512]{1,0:T(8,128)(2,1)} %feat_hbm.1, s32[27,512]{1,0:T(8,128)} %bitcast.12, s32[1,512]{1,0:T(1,128)} %order_ref.1, s32[1,512]{1,0:T(1,128)} %bitcast.14, bf16[27,512,128]{2,1,0:T(8,128)(2,1)} %convw_hbm.1, f32[1,128]{1,0:T(1,128)} %bitcast.23, f32[1,512]{1,0:T(1,128)} %bitcast.15, ...), custom_call_target="tpu_custom_call" | custom-call | tf_op jit(solution)/shard_map/block/pallas_call | solution.py:536
  91.0 1.9 %copy.21 = bf16[512,512]{1,0:T(8,128)(2,1)} copy(bf16[512,512]{1,0:T(8,128)(2,1)} %block.1) | data formatting | bytes 1048576
